TPU v7x, 32 devices: a whole 2x2x4 slice. The times are simulated.
32 devices in a mesh: dp: 16 (over z, y, core), tensor: 2 (over x).
Axes of the slice: x: 2, y: 2, z: 4, core: 2. Of those that a mesh axis runs over, the one named last changes fastest.
Arguments:
- resid_in: float32 [8192, 1024], P(('dp', 'tensor')), may hold values from -6 to 6
- segments: int32 [8192], P('dp'), may hold values from 0 to 15, never falling along the last dimension, each value on 1 to 1024 neighbouring positions
- cotangent: float32 [8192, 1024], P(('dp', 'tensor')), may hold values from -6 to 6
- norm_gain: float32 [2, 1024], replicated, may hold values from 0.25 to 1.75
- inner_proj: bfloat16 [2, 1024, 2, 2048], P(None, 'dp', None, 'tensor'), may hold values from -0.1875 to 0.1875
- shared_proj: bfloat16 [2, 1024, 288], replicated, may hold values from -0.1875 to 0.1875
- conv_weight: float32 [2, 4, 2304], replicated, may hold values from -3 to 3
- conv_bias: float32 [2, 2304], replicated, may hold values from -0.5 to 0.5
- dt_offset: float32 [2, 32], replicated, may hold values from -5 to -2
- rate_log: float32 [2, 32], replicated, may hold values from -2 to 2.5
- skip_gain: float32 [2, 32], replicated, may hold values from 0.5 to 1.5
- mix_gain: float32 [2, 2048], replicated, may hold values from 0.25 to 1.75
- out_proj: bfloat16 [2, 2048, 1024], P(None, 'tensor', 'dp'), may hold values from -0.125 to 0.125
Outputs:
- resid_out: float32 [8192, 1024], P(('dp', 'tensor'))
- grad_in: float32 [8192, 1024], P(('dp', 'tensor'))
- grad_norm_gain: float32 [2, 1024], replicated
- grad_inner_proj: float32 [2, 1024, 2, 2048], P(None, 'dp', None, 'tensor')
- grad_shared_proj: float32 [2, 1024, 288], replicated
- grad_conv_weight: float32 [2, 4, 2304], replicated
- grad_conv_bias: float32 [2, 2304], replicated
- grad_dt_offset: float32 [2, 32], replicated
- grad_rate_log: float32 [2, 32], replicated
- grad_skip_gain: float32 [2, 32], replicated
- grad_mix_gain: float32 [2, 2048], replicated
- grad_out_proj: float32 [2, 2048, 1024], P(None, 'tensor', 'dp')
Inputs may be any that keep to these rules, and one draw needn't show every extreme that they name: `segments`: segment numbers never fall along the tokens; each segment covers 1 to 1024 consecutive tokens.
All inputs are finite; a program needn't handle non-finite values.
Results may differ from a plain program's by a relative error of at most 0.012.
Values may be sent and summed in bfloat16 or wider, within the bound.
A program may use at most 192 MiB of HBM per device.

v0:
```python
import jax
import jax.numpy as jnp
from jax import lax
from jax.sharding import PartitionSpec as P

D = 1024
HEADS = 32
HEADDIM = 64
STATE = 128
KCONV = 4
BLOCK = 256
INNER = 2048


epsilon = 1e-05
precise = lax.Precision.HIGHEST


def causal_conv(values, weight, offset, segment):
    length = values.shape[0]
    tap_count = weight.shape[0]
    summed = offset[None, :] + weight[tap_count - 1][None, :] * values
    for lag_steps in range(1, tap_count):
        shifted = jnp.concatenate(
            [jnp.zeros((lag_steps, values.shape[1]), values.dtype), values[: length - lag_steps]],
            axis=0,
        )
        earlier = jnp.concatenate(
            [jnp.full((lag_steps,), -1, jnp.int32), segment[: length - lag_steps]], axis=0
        )
        joined = (earlier == segment).astype(values.dtype)
        summed = summed + weight[tap_count - 1 - lag_steps][None, :] * shifted * joined[:, None]
    return summed


def state_space(x_heads, step_sizes, rates, b_rows, c_rows, segment, skip_gains):
    length, head_count, head_width = x_heads.shape
    blocks = length // BLOCK
    float_type = x_heads.dtype
    log_decay = -(step_sizes * rates[None, :])
    cumulative = jnp.transpose(
        jnp.cumsum(log_decay.reshape(blocks, BLOCK, head_count), axis=1), (0, 2, 1)
    )
    step_blocks = jnp.transpose(step_sizes.reshape(blocks, BLOCK, head_count), (0, 2, 1))
    seg_blocks = segment.reshape(blocks, BLOCK)
    x_blocks = x_heads.reshape(blocks, BLOCK, head_count, head_width)
    b_blocks = b_rows.reshape(blocks, BLOCK, -1)
    c_blocks = c_rows.reshape(blocks, BLOCK, -1)
    positions = lax.iota(jnp.int32, BLOCK)
    causal = positions[:, None] >= positions[None, :]
    linked = (seg_blocks[:, :, None] == seg_blocks[:, None, :]) & causal[None]
    log_gap = cumulative[:, :, :, None] - cumulative[:, :, None, :]
    decays = jnp.exp(jnp.where(linked[:, None], log_gap, 0.0)) * linked[:, None].astype(float_type)
    pairing = jnp.einsum("kin,kjn->kij", c_blocks, b_blocks, precision=precise)
    mixing = pairing[:, None] * decays * step_blocks[:, :, None, :]
    inside = jnp.einsum("khij,kjhp->kihp", mixing, x_blocks, precision=precise)
    last_seg = seg_blocks[:, -1]
    same_end = (seg_blocks == last_seg[:, None]).astype(float_type)
    to_end = jnp.exp(cumulative[:, :, -1:] - cumulative) * same_end[:, None, :] * step_blocks
    weighted_x = x_blocks * jnp.transpose(to_end, (0, 2, 1))[:, :, :, None]
    block_states = jnp.einsum("kjn,kjhp->khnp", b_blocks, weighted_x, precision=precise)
    prior_seg = jnp.concatenate([jnp.full((1,), -1, jnp.int32), last_seg[:-1]])
    carry_on = (last_seg == prior_seg).astype(float_type)
    totals = jnp.exp(cumulative[:, :, -1])

    def advance(running, pieces):
        block_state, block_total, block_keep = pieces
        return (running * (block_total * block_keep)[:, None, None] + block_state, running)

    unused, entering = lax.scan(
        advance, jnp.zeros(block_states.shape[1:], float_type), (block_states, totals, carry_on)
    )
    reaches = (
        jnp.exp(cumulative) * (seg_blocks == prior_seg[:, None]).astype(float_type)[:, None, :]
    )
    carried = jnp.einsum("kin,khnp->kihp", c_blocks, entering, precision=precise)
    carried = carried * jnp.transpose(reaches, (0, 2, 1))[:, :, :, None]
    result = inside + carried + skip_gains[None, None, :, None] * x_blocks
    return result.reshape(length, head_count * head_width)


def mixer_sequence(
    z_part,
    x_part,
    bc_raw,
    dt_raw,
    conv_x_weight,
    conv_x_offset,
    conv_bc_weight,
    conv_bc_offset,
    dt_shift,
    rate_logs,
    skip_gains,
    segment,
):
    length = x_part.shape[0]
    x_conv = jax.nn.silu(causal_conv(x_part, conv_x_weight, conv_x_offset, segment))
    bc_conv = jax.nn.silu(causal_conv(bc_raw, conv_bc_weight, conv_bc_offset, segment))
    step_sizes = jax.nn.softplus(dt_raw + dt_shift[None, :])
    rates = jnp.exp(rate_logs)
    mixed = state_space(
        x_conv.reshape(length, -1, HEADDIM),
        step_sizes,
        rates,
        bc_conv[:, :STATE],
        bc_conv[:, STATE:],
        segment,
        skip_gains,
    )
    return mixed * jax.nn.silu(z_part)


def rows_product(left_rows, right_matrix):
    return jnp.dot(left_rows, right_matrix, preferred_element_type=jnp.float32)


def fetch_weights(inner_rows, out_cols):
    return (
        lax.all_gather(inner_rows, "dp", axis=0, tiled=True),
        lax.all_gather(out_cols, "dp", axis=1, tiled=True),
    )


def place_slot(piece, full_shape, start, axis_pos):
    return lax.dynamic_update_slice_in_dim(
        jnp.zeros(full_shape, jnp.float32), piece, start, axis_pos
    )


def on_device(
    resid_in,
    segments,
    cotangent,
    norm_gain,
    inner_proj,
    shared_proj,
    conv_weight,
    conv_bias,
    dt_offset,
    rate_log,
    skip_gain,
    mix_gain,
    out_proj,
):
    tensor_index = lax.axis_index("tensor")
    local_inner = inner_proj.shape[3]
    local_heads = local_inner // HEADDIM
    seq_rows = segments.shape[0]
    layer_count = norm_gain.shape[0]
    inner_start = tensor_index * local_inner
    head_start = tensor_index * local_heads

    def mixer_core(
        inner_part,
        bc_raw,
        dt_raw,
        conv_x_weight,
        conv_x_offset,
        conv_bc_weight,
        conv_bc_offset,
        dt_shift,
        rate_logs,
        skip_gains,
    ):
        return mixer_sequence(
            inner_part[:, 0],
            inner_part[:, 1],
            bc_raw,
            dt_raw,
            conv_x_weight,
            conv_x_offset,
            conv_bc_weight,
            conv_bc_offset,
            dt_shift,
            rate_logs,
            skip_gains,
            segments,
        )

    stored = []
    residual = resid_in
    for layer_pos in range(layer_count):
        gain_in = norm_gain[layer_pos]
        inv_in = lax.rsqrt(jnp.mean(residual * residual, axis=1) + epsilon)
        normed_rows = (residual * inv_in[:, None] * gain_in[None, :]).astype(jnp.bfloat16)
        normed_all = lax.all_gather(normed_rows, "tensor", axis=0, tiled=True)
        inner_w, out_w = fetch_weights(inner_proj[layer_pos], out_proj[layer_pos])
        inner_flat = inner_w.reshape(inner_w.shape[0], 2 * local_inner)
        shared_w = shared_proj[layer_pos]
        inner_out = jnp.dot(normed_all, inner_flat, preferred_element_type=jnp.float32).reshape(
            seq_rows, 2, local_inner
        )
        shared_out = jnp.dot(normed_all, shared_w, preferred_element_type=jnp.float32)
        conv_layer = conv_weight[layer_pos]
        offset_layer = conv_bias[layer_pos]
        mix_pre, mixer_back = jax.vjp(
            jax.checkpoint(mixer_core),
            inner_out,
            shared_out[:, : 2 * STATE],
            lax.dynamic_slice_in_dim(shared_out, 2 * STATE + head_start, local_heads, 1),
            lax.dynamic_slice_in_dim(conv_layer, inner_start, local_inner, 1),
            lax.dynamic_slice_in_dim(offset_layer, inner_start, local_inner, 0),
            conv_layer[:, INNER:],
            offset_layer[INNER:],
            lax.dynamic_slice_in_dim(dt_offset[layer_pos], head_start, local_heads, 0),
            lax.dynamic_slice_in_dim(rate_log[layer_pos], head_start, local_heads, 0),
            lax.dynamic_slice_in_dim(skip_gain[layer_pos], head_start, local_heads, 0),
        )
        record = {
            "residual": residual,
            "inv_in": inv_in,
            "normed_rows": normed_rows,
            "normed_all": normed_all,
            "inner_w": inner_w,
            "out_w": out_w,
            "mixer_back": mixer_back,
        }
        mix_local = lax.dynamic_slice_in_dim(mix_gain[layer_pos], inner_start, local_inner, 0)
        squares = lax.psum(jnp.sum(mix_pre * mix_pre, axis=1), "tensor")
        inv_mix = lax.rsqrt(squares / INNER + epsilon)
        gated_low = (mix_pre * inv_mix[:, None] * mix_local[None, :]).astype(jnp.bfloat16)
        branch = lax.psum_scatter(
            rows_product(gated_low, out_w), "tensor", scatter_dimension=0, tiled=True
        )
        record["mix_pre"] = mix_pre
        record["mix_local"] = mix_local
        record["inv_mix"] = inv_mix
        record["gated_low"] = gated_low
        stored.append(record)
        residual = residual + branch
    layer_output = residual
    grad_resid = cotangent
    per_layer = [None] * layer_count
    for layer_pos in reversed(range(layer_count)):
        record = stored[layer_pos]
        inner_w, out_w = fetch_weights(inner_proj[layer_pos], out_proj[layer_pos])
        inner_flat = inner_w.reshape(inner_w.shape[0], 2 * local_inner)
        shared_w = shared_proj[layer_pos]
        inv_mix = record["inv_mix"]
        gated_low = record["gated_low"]
        grad_branch = grad_resid.astype(jnp.bfloat16)
        mix_pre = record["mix_pre"]
        grad_all = lax.all_gather(grad_branch, "tensor", axis=0, tiled=True)
        grad_gated = jnp.einsum("gd,cd->gc", grad_all, out_w, preferred_element_type=jnp.float32)
        grad_out = jnp.einsum("gc,gd->cd", gated_low, grad_all, preferred_element_type=jnp.float32)
        scaled = grad_gated * record["mix_local"][None, :]
        grad_mix = place_slot(
            jnp.sum(grad_gated * mix_pre * inv_mix[:, None], axis=0), (INNER,), inner_start, 0
        )
        inner_dot = lax.psum(jnp.sum(scaled * mix_pre, axis=1), "tensor")
        cubed = inv_mix * inv_mix * inv_mix
        grad_mix_pre = scaled * inv_mix[:, None] - mix_pre * (cubed * inner_dot / INNER)[:, None]
        (
            grad_inner_out,
            grad_bc,
            grad_dt,
            grad_conv_x,
            grad_offset_x,
            grad_conv_bc,
            grad_offset_bc,
            grad_shift,
            grad_rates,
            grad_skips,
        ) = record["mixer_back"](grad_mix_pre)
        grad_inner_low = grad_inner_out.astype(jnp.bfloat16).reshape(seq_rows, 2 * local_inner)
        grad_dt_full = place_slot(grad_dt, (seq_rows, HEADS), head_start, 1)
        grad_shared_all = jnp.concatenate([grad_bc, grad_dt_full], axis=1)
        grad_in_part = jnp.einsum(
            "gk,dk->gd", grad_inner_low, inner_flat, preferred_element_type=jnp.float32
        )
        grad_rows, grad_shared_rows = (
            lax.psum_scatter(grad_in_part, "tensor", scatter_dimension=0, tiled=True),
            lax.psum_scatter(grad_shared_all, "tensor", scatter_dimension=0, tiled=True),
        )
        grad_shared_low = grad_shared_rows.astype(jnp.bfloat16)
        normed_rows = record["normed_rows"]
        grad_normed = grad_rows + jnp.einsum(
            "rk,dk->rd", grad_shared_low, shared_w, preferred_element_type=jnp.float32
        )
        grad_shared_w = jnp.einsum(
            "rd,rk->dk", normed_rows, grad_shared_low, preferred_element_type=jnp.float32
        )
        grad_inner = jnp.einsum(
            "gd,gk->dk", record["normed_all"], grad_inner_low, preferred_element_type=jnp.float32
        ).reshape(-1, 2, local_inner)
        residual = record["residual"]
        inv_in = record["inv_in"]
        gain_in = norm_gain[layer_pos]
        weighted = grad_normed * gain_in[None, :]
        grad_gain_in = jnp.sum(grad_normed * residual * inv_in[:, None], axis=0)
        input_dot = jnp.sum(weighted * residual, axis=1)
        cubed_in = inv_in * inv_in * inv_in
        grad_resid = (
            grad_resid + weighted * inv_in[:, None] - residual * (cubed_in * input_dot / D)[:, None]
        )
        inner_shard, out_shard = (
            lax.psum_scatter(grad_inner, "dp", scatter_dimension=0, tiled=True),
            lax.psum_scatter(grad_out, "dp", scatter_dimension=1, tiled=True),
        )
        conv_grad = jnp.concatenate(
            [place_slot(grad_conv_x, (KCONV, INNER), inner_start, 1), grad_conv_bc], axis=1
        )
        offset_grad = jnp.concatenate(
            [place_slot(grad_offset_x, (INNER,), inner_start, 0), grad_offset_bc], axis=0
        )
        small_sums = lax.psum(
            (
                grad_gain_in,
                grad_shared_w,
                conv_grad,
                offset_grad,
                place_slot(grad_shift, (HEADS,), head_start, 0),
                place_slot(grad_rates, (HEADS,), head_start, 0),
                place_slot(grad_skips, (HEADS,), head_start, 0),
                grad_mix,
            ),
            ("dp", "tensor"),
        )
        per_layer[layer_pos] = (
            small_sums[0],
            inner_shard,
            small_sums[1],
            small_sums[2],
            small_sums[3],
            small_sums[4],
            small_sums[5],
            small_sums[6],
            small_sums[7],
            out_shard,
        )
    stacked = [
        jnp.stack([per_layer[layer_pos][member] for layer_pos in range(layer_count)], axis=0)
        for member in range(10)
    ]
    return (
        layer_output,
        grad_resid,
        stacked[0],
        stacked[1],
        stacked[2],
        stacked[3],
        stacked[4],
        stacked[5],
        stacked[6],
        stacked[7],
        stacked[8],
        stacked[9],
    )


def solution(mesh):
    in_specs = (
        P(("dp", "tensor"), None),
        P("dp"),
        P(("dp", "tensor"), None),
        P(),
        P(None, "dp", None, "tensor"),
        P(),
        P(),
        P(),
        P(),
        P(),
        P(),
        P(),
        P(None, "tensor", "dp"),
    )
    out_specs = (
        P(("dp", "tensor"), None),
        P(("dp", "tensor"), None),
        P(),
        P(None, "dp", None, "tensor"),
        P(),
        P(),
        P(),
        P(),
        P(),
        P(),
        P(),
        P(None, "tensor", "dp"),
    )
    return jax.shard_map(
        on_device, mesh=mesh, in_specs=in_specs, out_specs=out_specs, check_vma=False
    )
```

profile of v0, /device:TPU:0, one launch (start us, length us, event | category | flops | bytes accessed | tf_op | source)
XLA Modules:
  0.0 1636.3 jit_solution(3401382363175636471)
XLA Ops:
  24.2 11.8 all-gather.13.cloned.1.call-done
  48.2 41.2 %all-gather.21.cloned.1.call-done = bf16[1,1024,2,1024]{3,1,2,0:T(8,128)(2,1)} async-done(((bf16[1,64,2,1024]{3,1,2,0:T(8,128)(2,1)}), bf16[1,1024,2,1024]{3,1,2,0:T(8,128)(2,1)}) %all-gather.21.cloned.1.call-update) | async-done | bytes 4194320 | tf_op jit(solution)/shard_map/all_gather | solution.py:119
  134.1 11.3 multiply_reduce_fusion.21
  169.1 28.6 %reduce-scatter.11.cloned.1.call-done = f32[256,1024]{1,0:T(8,128)} async-done(((f32[512,1024]{1,0:T(8,128)}), f32[256,1024]{1,0:T(8,128)}) %reduce-scatter.11.cloned.1.call-update) | async-done | bytes 1048592 | tf_op jit(solution)/shard_map/reduce_scatter | solution.py:222
  207.4 43.8 %all-gather.25.cloned.1.call-done = bf16[1,1024,2,1024]{3,1,2,0:T(8,128)(2,1)} async-done(((bf16[1,64,2,1024]{3,1,2,0:T(8,128)(2,1)}), bf16[1,1024,2,1024]{3,1,2,0:T(8,128)(2,1)}) %all-gather.25.cloned.1.call-update) | async-done | bytes 4194320 | tf_op jit(solution)/shard_map/all_gather | solution.py:119
  257.6 14.9 all-gather.15.cloned.1.call-done
  323.1 11.6 while.99
  338.1 11.4 multiply_reduce_fusion.20
  450.4 12.5 while.101
  483.7 16.0 fusion.41
  533.1 11.7 bitcast_add_fusion.9
  609.2 26.0 %reduce-scatter.15.cloned.1.call-done = f32[256,1024]{1,0:T(8,128)} async-done(((f32[512,1024]{1,0:T(8,128)}), f32[256,1024]{1,0:T(8,128)}) %reduce-scatter.15.cloned.1.call-update) | async-done | bytes 1048592 | tf_op jit(solution)/shard_map/reduce_scatter | solution.py:272
  638.0 31.4 %reduce-scatter.13.cloned.1.call-done = f32[256,1024]{1,0:T(8,128)} async-done(((f32[512,1024]{1,0:T(8,128)}), f32[256,1024]{1,0:T(8,128)}) %reduce-scatter.13.cloned.1.call-update) | async-done | bytes 1048592 | tf_op jit(solution)/shard_map/reduce_scatter | solution.py:222
  674.6 19.4 %all-gather.19.cloned.1.call-done = bf16[512,1024]{1,0:T(8,128)(2,1)} async-done(((bf16[256,1024]{1,0:T(8,128)(2,1)}), bf16[512,1024]{1,0:T(8,128)(2,1)}) %all-gather.19.cloned.1.call-update) | async-done | bytes 1048592 | tf_op jit(solution)/shard_map/all_gather | solution.py:243
  753.4 18.1 %while.102 = (s32[]{:T(128)}, f32[16,128,64]{2,1,0:T(8,128)S(1)}, f32[2,16,128,64]{3,2,1,0:T(8,128)}, f32[2,16,1,1]{1,3,2,0:T(1,128)}, f32[2,16]{1,0:T(2,128)}, ...) while((s32[]{:T(128)}, f32[16,128,64]{2,1,0:T(8,128)S(1)}, ...), condition=%wide.region_42.44_spmd.clone, body=%wide.region_41.43_spmd.clone.sunk | while | flops 524323 | bytes 5245760 | solution.py:70
  796.0 13.9 while.103
  833.4 15.1 fusion.43
  948.8 25.4 %reduce-scatter.19.cloned.1.call-done = f32[256,1024]{1,0:T(8,128)} async-done(((f32[512,1024]{1,0:T(8,128)}), f32[256,1024]{1,0:T(8,128)}) %reduce-scatter.19.cloned.1.call-update) | async-done | bytes 1048592 | tf_op jit(solution)/shard_map/reduce_scatter | solution.py:272
  1012.6 102.7 %all-reduce.77.cloned.1.call-done = (f32[1,1024,288]{1,2,0:T(8,128)}, f32[1,1024,288]{1,2,0:T(8,128)}) async-done(((f32[1,1024,288]{1,2,0:T(8,128)}, f32[1,1024,288]{1,2,0:T(8,128)}), (f32[1,1024,288]{1,2,0:T(8,128)}, f32[1,1024,288]{1,2,0:T(8,128)})) %all-reduce.77.cloned.1.call-update) | async-done | bytes 2359312 | tf_op jit(solution)/shard_map/psum | solution.py:306
  1120.1 137.4 %all-reduce.75.cloned.1.call-done = (f32[1,1024]{1,0:T(1,128)}, f32[1,1024]{1,0:T(1,128)}, f32[1,4,2304]{2,1,0:T(4,128)}, f32[1,4,2304]{2,1,0:T(4,128)}, f32[1,2...) async-done(((f32[1,1024]{1,0:T(1,128)}, f32[1,1024]{1,0:T(1,128)}, ...) | async-done | bytes 117520 | tf_op jit(solution)/shard_map/psum | solution.py:306
  1266.5 67.3 %reduce-scatter.29.cloned.1.call-done = f32[1024,64]{0,1:T(8,128)} async-done(((f32[1024,1024]{0,1:T(8,128)}), f32[1024,64]{0,1:T(8,128)}) %reduce-scatter.29.cloned.1.call-update) | async-done | bytes 262160 | tf_op jit(solution)/shard_map/reduce_scatter | solution.py:298
  1333.8 75.2 %reduce-scatter.27.cloned.1.call-done = f32[1024,64]{0,1:T(8,128)} async-done(((f32[1024,1024]{0,1:T(8,128)}), f32[1024,64]{0,1:T(8,128)}) %reduce-scatter.27.cloned.1.call-update) | async-done | bytes 262160 | tf_op jit(solution)/shard_map/reduce_scatter | solution.py:298
  1410.9 106.5 %reduce-scatter.25.cloned.1.call-done = f32[64,2,1024]{2,0,1:T(8,128)} async-done(((f32[1024,2,1024]{2,0,1:T(8,128)}), f32[64,2,1024]{2,0,1:T(8,128)}) %reduce-scatter.25.cloned.1.call-update) | async-done | bytes 524304 | tf_op jit(solution)/shard_map/reduce_scatter | solution.py:297
  1517.3 108.9 %reduce-scatter.23.cloned.1.call-done = f32[64,2,1024]{2,0,1:T(8,128)} async-done(((f32[1024,2,1024]{2,0,1:T(8,128)}), f32[64,2,1024]{2,0,1:T(8,128)}) %reduce-scatter.23.cloned.1.call-update) | async-done | bytes 524304 | tf_op jit(solution)/shard_map/reduce_scatter | solution.py:297
  (1114 shorter events, 728.0 us)
Async XLA Ops:
  7.2 28.8 %all-gather.13.cloned.1.call-start = ((), (), s32[]{:S(2)}) async-start(), calls=%async_computation.10 | async-start | bytes 1572864 | tf_op jit(solution)/shard_map/all_gather | solution.py:186
  8.0 191.7 %copy-start.128 = (f32[1,1024]{1,0:T(1,128)}, f32[1,1024]{1,0:T(1,128)S(1)}, u32[]{:S(2)}) copy-start(f32[1,1024]{1,0:T(1,128)S(1)} %get-tuple-element.1244) | copy-start | bytes 12292
  11.8 77.5 %all-gather.21.cloned.1.call-start = ((), (), s32[]{:S(2)}) async-start(), calls=%async_computation.24 | async-start | bytes 4456448 | tf_op jit(solution)/shard_map/all_gather | solution.py:119
  13.7 148.0 %all-gather.23.cloned.1.call-start = ((), (), s32[]{:S(2)}) async-start(), calls=%async_computation.25 | async-start | bytes 2228224 | tf_op jit(solution)/shard_map/all_gather | solution.py:120
  14.5 183.1 %reduce-scatter.11.cloned.1.call-start = ((), (), s32[]{:S(2)}) async-start(), calls=%async_computation.11 | async-start | bytes 3145728 | tf_op jit(solution)/shard_map/reduce_scatter | solution.py:222
  22.8 77.9 %copy-start.152 = (f32[1,1024]{1,0:T(1,128)}, f32[1,1024]{1,0:T(1,128)S(1)}, u32[]{:S(2)}) copy-start(f32[1,1024]{1,0:T(1,128)S(1)} %constant_dynamic-slice_fusion.31) | copy-start | bytes 12292
  23.4 138.3 %copy-start.104 = (f32[1,1024]{1,0:T(1,128)}, f32[1,1024]{1,0:T(1,128)S(1)}, u32[]{:S(2)}) copy-start(f32[1,1024]{1,0:T(1,128)S(1)} %constant_dynamic-slice_fusion.26) | copy-start | bytes 12292
  23.5 258.5 %copy-start.132 = (f32[512]{0:T(512)}, f32[512]{0:T(512)S(1)}, u32[]{:S(2)}) copy-start(f32[512]{0:T(512)S(1)} %get-tuple-element.1268) | copy-start | bytes 6148
  167.3 83.9 %all-gather.25.cloned.1.call-start = ((), (), s32[]{:S(2)}) async-start(), calls=%async_computation.26 | async-start | bytes 4456448 | tf_op jit(solution)/shard_map/all_gather | solution.py:119
  169.0 103.4 %all-gather.15.cloned.1.call-start = ((), (), s32[]{:S(2)}) async-start(), calls=%async_computation.12 | async-start | bytes 1572864 | tf_op jit(solution)/shard_map/all_gather | solution.py:186
  201.1 162.0 %all-gather.17.cloned.1.call-start = ((), (), s32[]{:S(2)}) async-start(), calls=%async_computation.14 | async-start | bytes 1572864 | tf_op jit(solution)/shard_map/all_gather | solution.py:243
  202.1 161.0 %all-gather.27.cloned.1.call-start = ((), (), s32[]{:S(2)}) async-start(), calls=%async_computation.27 | async-start | bytes 2228224 | tf_op jit(solution)/shard_map/all_gather | solution.py:120
  202.8 406.4 %reduce-scatter.17.cloned.1.call-start = ((), (), s32[]{:S(2)}) async-start(), calls=%async_computation.16 | async-start | bytes 884736 | tf_op jit(solution)/shard_map/reduce_scatter | solution.py:273
  533.0 102.2 %reduce-scatter.15.cloned.1.call-start = ((), (), s32[]{:S(2)}) async-start(), calls=%async_computation.15 | async-start | bytes 3145728 | tf_op jit(solution)/shard_map/reduce_scatter | solution.py:272
  603.3 66.2 %reduce-scatter.13.cloned.1.call-start = ((), (), s32[]{:S(2)}) async-start(), calls=%async_computation.13 | async-start | bytes 3145728 | tf_op jit(solution)/shard_map/reduce_scatter | solution.py:222
  609.1 84.8 %all-gather.19.cloned.1.call-start = ((), (), s32[]{:S(2)}) async-start(), calls=%async_computation.17 | async-start | bytes 1572864 | tf_op jit(solution)/shard_map/all_gather | solution.py:243
  672.5 272.4 %reduce-scatter.21.cloned.1.call-start = ((), (), s32[]{:S(2)}) async-start(), calls=%async_computation.19 | async-start | bytes 884736 | tf_op jit(solution)/shard_map/reduce_scatter | solution.py:273
  924.1 50.1 %reduce-scatter.19.cloned.1.call-start = ((), (), s32[]{:S(2)}) async-start(), calls=%async_computation.18 | async-start | bytes 3145728 | tf_op jit(solution)/shard_map/reduce_scatter | solution.py:272
  937.8 177.5 %all-reduce.77.cloned.1.call-start = ((), (), s32[]{:S(2)}) async-start(), calls=%async_computation.29 | async-start | bytes 4718592 | tf_op jit(solution)/shard_map/psum | solution.py:306
  947.3 310.1 %all-reduce.75.cloned.1.call-start = ((), (), s32[]{:S(2)}) async-start(), calls=%async_computation.28 | async-start | bytes 239616 | tf_op jit(solution)/shard_map/psum | solution.py:306
  977.8 356.0 %reduce-scatter.29.cloned.1.call-start = ((), (), s32[]{:S(2)}) async-start(), calls=%async_computation.23 | async-start | bytes 4456448 | tf_op jit(solution)/shard_map/reduce_scatter | solution.py:298
  982.5 426.5 %reduce-scatter.27.cloned.1.call-start = ((), (), s32[]{:S(2)}) async-start(), calls=%async_computation.22 | async-start | bytes 4456448 | tf_op jit(solution)/shard_map/reduce_scatter | solution.py:298
  988.8 528.6 %reduce-scatter.25.cloned.1.call-start = ((), (), s32[]{:S(2)}) async-start(), calls=%async_computation.21 | async-start | bytes 8912896 | tf_op jit(solution)/shard_map/reduce_scatter | solution.py:297
  1000.8 625.4 %reduce-scatter.23.cloned.1.call-start = ((), (), s32[]{:S(2)}) async-start(), calls=%async_computation.20 | async-start | bytes 8912896 | tf_op jit(solution)/shard_map/reduce_scatter | solution.py:297
  (294 other events, 2094.5 us)
Sparse Core Ops, SparseCore 0:
  11.9 23.9 all-gather.12
  38.7 50.5 all-gather.20
  91.5 39.8 all-gather.22
  167.4 30.2 reduce-scatter.10
  200.5 50.5 all-gather.24
  252.6 19.7 all-gather.14
  274.1 21.2 all-gather.16
  297.8 41.4 all-gather.26
  533.2 15.2 reduce-scatter.16
  603.4 31.7 reduce-scatter.14
  637.6 31.8 reduce-scatter.12
  672.6 21.3 all-gather.18
  924.2 15.2 reduce-scatter.20
  942.3 31.8 reduce-scatter.18
  979.7 135.5 all-reduce.76
  1123.9 133.5 all-reduce.74
  1261.6 72.1 reduce-scatter.28
  1337.5 71.4 reduce-scatter.26
  1413.6 103.6 reduce-scatter.24
  1521.8 104.3 reduce-scatter.22
where the time goes:
time: 1640 us
  waiting for transfers between devices  841 us (51%)
  local copies, waits for them, and re-layouts  284 us (17%)
  matrix products  272 us (17%)
  other arithmetic  200 us (12%)
  blocking collectives  19.7 us (1%)
  between operations  17.6 us (1%)
    psum x2, waiting for transfers between devices, on_device(): lax.psum((grad_gain_in, grad_shared_w, conv_grad, offset_grad, place_slot...  240 us
    reduce_scatter x2, waiting for transfers between devices, on_device(): lax.psum_scatter(grad_inner, 'dp', scatter_dimension=0, tiled=True)  215 us
    reduce_scatter x2, waiting for transfers between devices, on_device(): lax.psum_scatter(grad_out, 'dp', scatter_dimension=1, tiled=True)  142 us
    dot_general x8, matrix products, state_space(): inside = jnp.einsum('khij,kjhp->kihp', mixing, x_blocks, precision=precise)  95.9 us
    all_gather x2, waiting for transfers between devices, fetch_weights(): lax.all_gather(inner_rows, 'dp', axis=0, tiled=True)  85 us
    reduce_scatter x2, waiting for transfers between devices, on_device(): lax.psum_scatter(rows_product(gated_low, out_w), 'tensor', scatter_dimens...  60.1 us
    reduce_scatter x2, waiting for transfers between devices, on_device(): lax.psum_scatter(grad_in_part, 'tensor', scatter_dimension=0, tiled=True)  51.4 us
    dot_general x8, matrix products, state_space(): jnp.einsum('kjn,kjhp->khnp', b_blocks, weighted_x, precision=precise)  46.4 us
  transfers between devices with their start and end apart: 20, of which 15 were waited for; matrix products, arithmetic and copies ran while one was open for 20% of the time, Pallas kernels for 0%

commit v1 on v0

v1 whole, which is shorter than its diff:
```python
import jax
import jax.numpy as jnp
from jax import lax
from jax.experimental import pallas as pl
from jax.experimental.pallas import tpu as pltpu
from jax.sharding import PartitionSpec as P

D = 1024
HEADS = 32
HEADDIM = 64
STATE = 128
KCONV = 4
INNER = 2048
LANES = 128
ROWS = 128
SIDE = 3 * LANES

epsilon = 1e-05
precise = lax.Precision.HIGHEST
f32 = jnp.float32
bf16 = jnp.bfloat16


def dot(a, b, ca=1, cb=0, precision=None):
    return lax.dot_general(
        a, b, (((ca,), (cb,)), ((), ())), precision=precision, preferred_element_type=f32
    )


def sigmoid(a):
    return 1.0 / (1.0 + jnp.exp(-a))


def conv_rows(values, cols, weights):
    total = weights[4:5] + weights[3:4] * values
    for lag in range(1, KCONV):
        total = total + weights[3 - lag : 4 - lag] * (
            pltpu.roll(values, lag, 0) * cols[:, lag - 1 : lag]
        )
    return total


def conv_rows_back(gconv, values, cols, weights):
    length = values.shape[0]
    back = weights[3:4] * gconv
    taps = [None] * KCONV
    taps[3] = jnp.sum(gconv * values, axis=0, keepdims=True)
    for lag in range(1, KCONV):
        kept = gconv * cols[:, lag - 1 : lag]
        back = back + weights[3 - lag : 4 - lag] * pltpu.roll(kept, length - lag, 0)
        taps[3 - lag] = jnp.sum(kept * pltpu.roll(values, lag, 0), axis=0, keepdims=True)
    return back, taps + [jnp.sum(gconv, axis=0, keepdims=True)]


def iotas(shape):
    return lax.broadcasted_iota(jnp.int32, shape, 0), lax.broadcasted_iota(jnp.int32, shape, 1)


def row_blocks(length):
    return [(start, start + ROWS) for start in range(0, length, ROWS)]


def running_sum(values):
    row, col = iotas((ROWS, ROWS))
    lower = (row >= col).astype(f32)
    carry, parts = jnp.zeros((1, values.shape[1]), f32), []
    for start, stop in row_blocks(values.shape[0]):
        parts.append(dot(lower, values[start:stop], precision=precise) + carry)
        carry = parts[-1][ROWS - 1 : ROWS]
    return jnp.concatenate(parts, axis=0)


def running_sum_back(values):
    row, col = iotas((ROWS, ROWS))
    upper = (row <= col).astype(f32)
    carry, parts = jnp.zeros((1, values.shape[1]), f32), []
    for start, stop in reversed(row_blocks(values.shape[0])):
        parts.append(dot(upper, values[start:stop], precision=precise) + carry)
        carry = parts[-1][0:1]
    return jnp.concatenate(parts[::-1], axis=0)


def linked_later(cols_ref, segrow_ref, start, stop):
    row, col = iotas((stop - start, segrow_ref.shape[1] - start))
    return (row <= col) & (cols_ref[start:stop, 3:4] == segrow_ref[0:1, start:])


def step_sizes_of(shared_ref, heads_ref):
    pre = shared_ref[:, 2 * STATE :] + heads_ref[0:1]
    return pre, jnp.maximum(pre, 0.0) + jnp.log1p(jnp.exp(-jnp.abs(pre)))


def column_of(array, head):
    lane = lax.broadcasted_iota(jnp.int32, array.shape, 1)
    return jnp.sum(jnp.where(lane == head, array, 0.0), axis=1, keepdims=True)


def forward_kernel(
    z_ref, x_ref, shared_ref, cols_ref, segrow_ref, chan_ref, side_ref, heads_ref,
    y_ref, mix_ref,
    pair_ref, b_ref, c_ref, dt_ref, cum_ref, cumt_ref,
):
    step = pl.program_id(0)
    length = z_ref.shape[0]
    kept = pairs_kept(length)

    def pairs(start, stop):
        row, col = iotas((ROWS, stop))
        linked = (row + start >= col) & (cols_ref[start:stop, 3:4] == segrow_ref[0:1, :stop])
        return jnp.where(linked, dot(c_ref[start:stop], b_ref[:stop], 1, 1), 0.0)

    @pl.when(step == 0)
    def _():
        conv = conv_rows(shared_ref[:, : 2 * STATE], cols_ref[...], side_ref[...])
        bc = (conv * sigmoid(conv)).astype(bf16)
        b_ref[...] = bc[:, :STATE]
        c_ref[...] = bc[:, STATE:]
        for start, stop in row_blocks(length) if kept else []:
            pair_ref[start:stop, :stop] = pairs(start, stop)
        dt = step_sizes_of(shared_ref, heads_ref)[1]
        dt_ref[...] = dt
        cum = running_sum(-dt * heads_ref[1:2])
        cum_ref[...] = cum
        cumt_ref[...] = cum.T

    conv = conv_rows(x_ref[...], cols_ref[...], chan_ref[...])
    xs = conv * sigmoid(conv)
    z = z_ref[...]
    halves = []
    for half in range(LANES // HEADDIM):
        head = step * (LANES // HEADDIM) + half
        cumcol = column_of(cum_ref[...], head)
        cumrow = cumt_ref[pl.ds(head, 1), :]
        xdt = xs[:, half * HEADDIM : (half + 1) * HEADDIM] * column_of(dt_ref[...], head)
        xdt = xdt.astype(bf16)
        parts = []
        for start, stop in row_blocks(length):
            decay = jnp.exp(jnp.minimum(cumcol[start:stop] - cumrow[:, :stop], 0.0))
            pair = pair_ref[start:stop, :stop] if kept else pairs(start, stop)
            mixing = (pair * decay).astype(bf16)
            parts.append(dot(mixing, xdt[:stop]))
        halves.append(jnp.concatenate(parts, axis=0))
    y = jnp.concatenate(halves, axis=1) + chan_ref[6:7] * xs
    y_ref[...] = y
    mix_ref[...] = y * (z * sigmoid(z))


def backward_kernel(
    z_ref, x_ref, y_ref, gg_ref, shared_ref, cols_ref, segrow_ref, chan_ref, side_ref, heads_ref,
    gz_ref, gx_ref, gshared_ref, gchan_ref, gside_ref, gheads_ref,
    pair_ref, gpair_ref, gb_ref, gc_ref, b_ref, c_ref, dt_ref, cum_ref, cumt_ref, du_ref, mrow_ref,
):
    step = pl.program_id(0)
    length = z_ref.shape[0]
    kept = pairs_kept(length)

    def pairs(start, stop):
        linked = linked_later(cols_ref, segrow_ref, start, stop)
        return jnp.where(linked, dot(b_ref[start:stop], c_ref[start:], 1, 1), 0.0)

    def add_pair_grad(start, stop, gpair):
        linked = linked_later(cols_ref, segrow_ref, start, stop)
        gpair = jnp.where(linked, gpair, 0.0)
        gb_ref[start:stop] += dot(gpair.astype(bf16), c_ref[start:])
        gc_ref[start:] += dot(gpair.T.astype(bf16), b_ref[start:stop])

    @pl.when(step == 0)
    def _():
        conv = conv_rows(shared_ref[:, : 2 * STATE], cols_ref[...], side_ref[...])
        bc = (conv * sigmoid(conv)).astype(bf16)
        b_ref[...] = bc[:, :STATE]
        c_ref[...] = bc[:, STATE:]
        for start, stop in row_blocks(length) if kept else []:
            pair_ref[start:stop, start:] = pairs(start, stop)
            gpair_ref[start:stop, start:] = jnp.zeros((ROWS, length - start), f32)
        gb_ref[...] = jnp.zeros_like(gb_ref)
        gc_ref[...] = jnp.zeros_like(gc_ref)
        dt = step_sizes_of(shared_ref, heads_ref)[1]
        dt_ref[...] = dt
        cum = running_sum(-dt * heads_ref[1:2])
        cum_ref[...] = cum
        cumt_ref[...] = cum.T
        du_ref[...] = jnp.zeros_like(du_ref)
        mrow_ref[...] = jnp.zeros_like(mrow_ref)

    cols = cols_ref[...]
    x_raw = x_ref[...]
    conv = conv_rows(x_raw, cols, chan_ref[...])
    gate = sigmoid(conv)
    xs = conv * gate
    z = z_ref[...]
    zgate = sigmoid(z)
    zsilu = z * zgate
    y = y_ref[...]
    mix = y * zsilu
    gg = gg_ref[...]
    ggi = gg * cols[:, 4:5]
    gmix = ggi * chan_ref[5:6] - mix * cols[:, 5:6]
    ggain = jnp.sum(ggi * mix, axis=0, keepdims=True)
    gz_ref[...] = (gmix * y * (zgate * (1.0 + z * (1.0 - zgate)))).astype(bf16)
    gy = gmix * zsilu
    gskip = jnp.sum(xs * gy, axis=0, keepdims=True)
    xs_low, gy_low = xs.astype(bf16), gy.astype(bf16)
    halves = []
    for half in range(LANES // HEADDIM):
        head = step * (LANES // HEADDIM) + half
        span = slice(half * HEADDIM, (half + 1) * HEADDIM)
        cumcol = column_of(cum_ref[...], head)
        dtcol = column_of(dt_ref[...], head)
        cumrow = cumt_ref[pl.ds(head, 1), :]
        xh, gh = xs_low[:, span], gy_low[:, span]
        parts, dus = [], []
        mrow = jnp.zeros((1, length), f32)
        for start, stop in row_blocks(length):
            pair = pair_ref[start:stop, start:] if kept else pairs(start, stop)
            decay = jnp.exp(jnp.minimum(cumrow[:, start:] - cumcol[start:stop], 0.0))
            ga = decay * dot(xh[start:stop], gh[start:], 1, 1)
            u = pair * ga
            dtb = dtcol[start:stop]
            parts.append(dot((pair * decay).astype(bf16), gh[start:]) * dtb)
            if kept:
                gpair_ref[start:stop, start:] += ga * dtb
            else:
                add_pair_grad(start, stop, ga * dtb)
            dus.append(jnp.sum(u, axis=1, keepdims=True))
            sums = jnp.sum(u * dtb, axis=0, keepdims=True)
            if start:
                sums = jnp.concatenate([jnp.zeros((1, start), f32), sums], axis=1)
            mrow = mrow + sums
        halves.append(jnp.concatenate(parts, axis=0))
        mrow_ref[pl.ds(head, 1), :] = mrow
        lane = lax.broadcasted_iota(jnp.int32, du_ref.shape, 1)
        du_ref[...] = jnp.where(lane == head, jnp.concatenate(dus, axis=0), du_ref[...])
    gxs = jnp.concatenate(halves, axis=1) + chan_ref[6:7] * gy
    gconv = gxs * (gate * (1.0 + conv * (1.0 - gate)))
    gx, grows = conv_rows_back(gconv, x_raw, cols, chan_ref[...])
    gx_ref[...] = gx.astype(bf16)
    for place, value in enumerate(grows + [ggain, gskip]):
        gchan_ref[place : place + 1, :] = value
    gchan_ref[7:8, :] = jnp.zeros((1, LANES), f32)

    @pl.when(step == pl.num_programs(0) - 1)
    def _():
        for start, stop in row_blocks(length) if kept else []:
            add_pair_grad(start, stop, gpair_ref[start:stop, start:])
        raw = shared_ref[:, : 2 * STATE]
        conv = conv_rows(raw, cols_ref[...], side_ref[...])
        gate = sigmoid(conv)
        gconv = jnp.concatenate([gb_ref[...], gc_ref[...]], axis=1) * (gate * (1.0 + conv * (1.0 - gate)))
        graw, rows = conv_rows_back(gconv, raw, cols_ref[...], side_ref[...])
        gshared_ref[:, : 2 * STATE] = graw.astype(bf16)
        for place, value in enumerate(rows):
            gside_ref[place : place + 1, :] = value
        gside_ref[5:8, :] = jnp.zeros((3, 2 * STATE), f32)
        pre, dt = step_sizes_of(shared_ref, heads_ref)
        rate = heads_ref[1:2]
        du = du_ref[...]
        gcum = mrow_ref[...].T - du * dt
        later = running_sum_back(gcum)
        gdt = (du - rate * later) * sigmoid(pre)
        gshared_ref[:, 2 * STATE :] = gdt.astype(bf16)
        gheads_ref[0:1, :] = jnp.sum(gdt, axis=0, keepdims=True)
        gheads_ref[1:2, :] = -rate * jnp.sum(dt * later, axis=0, keepdims=True)
        gheads_ref[2:8, :] = jnp.zeros((6, LANES), f32)


def whole(shape):
    return pl.BlockSpec(shape, lambda i: (0, 0))


def lanes_block(rows, shift=0):
    return pl.BlockSpec((rows, LANES), lambda i: (0, i + shift))


def pairs_kept(length):
    return length <= 1024


def params():
    return pltpu.CompilerParams(
        vmem_limit_bytes=60 * 1024 * 1024, dimension_semantics=("arbitrary",)
    )


def mixer_forward(inner_out, shared_out, cols, segrow, chan, side, heads):
    length, width = inner_out.shape[0], inner_out.shape[1] // 2
    steps = width // LANES
    square = length if pairs_kept(length) else LANES
    return pl.pallas_call(
        forward_kernel,
        grid=(steps,),
        in_specs=[
            lanes_block(length), lanes_block(length, steps), whole((length, SIDE)),
            whole(cols.shape), whole(segrow.shape), lanes_block(8),
            whole(side.shape), whole(heads.shape),
        ],
        out_specs=[lanes_block(length)] * 2,
        out_shape=[jax.ShapeDtypeStruct((length, width), f32)] * 2,
        scratch_shapes=[
            pltpu.VMEM((square, square), f32),
            pltpu.VMEM((length, STATE), bf16),
            pltpu.VMEM((length, STATE), bf16),
            pltpu.VMEM((length, LANES), f32),
            pltpu.VMEM((length, LANES), f32),
            pltpu.VMEM((LANES, length), f32),
        ],
        compiler_params=params(),
        name="mixer_forward",
    )(inner_out, inner_out, shared_out, cols, segrow, chan, side, heads)


def mixer_backward(inner_out, y, grad_gated, shared_out, cols, segrow, chan, side, heads):
    length, width = y.shape
    steps = width // LANES
    square = length if pairs_kept(length) else LANES
    return pl.pallas_call(
        backward_kernel,
        grid=(steps,),
        in_specs=[
            lanes_block(length), lanes_block(length, steps), lanes_block(length),
            lanes_block(length), whole((length, SIDE)), whole(cols.shape),
            whole(segrow.shape), lanes_block(8), whole(side.shape), whole(heads.shape),
        ],
        out_specs=[
            lanes_block(length), lanes_block(length), whole((length, SIDE)),
            lanes_block(8), whole((8, 2 * STATE)), whole((8, LANES)),
        ],
        out_shape=[
            jax.ShapeDtypeStruct((length, width), bf16),
            jax.ShapeDtypeStruct((length, width), bf16),
            jax.ShapeDtypeStruct((length, SIDE), bf16),
            jax.ShapeDtypeStruct((8, width), f32),
            jax.ShapeDtypeStruct((8, 2 * STATE), f32),
            jax.ShapeDtypeStruct((8, LANES), f32),
        ],
        scratch_shapes=[
            pltpu.VMEM((square, square), f32),
            pltpu.VMEM((square, square), f32),
            pltpu.VMEM((length, STATE), f32),
            pltpu.VMEM((length, STATE), f32),
            pltpu.VMEM((length, STATE), bf16),
            pltpu.VMEM((length, STATE), bf16),
            pltpu.VMEM((length, LANES), f32),
            pltpu.VMEM((length, LANES), f32),
            pltpu.VMEM((LANES, length), f32),
            pltpu.VMEM((length, LANES), f32),
            pltpu.VMEM((LANES, length), f32),
        ],
        compiler_params=params(),
        name="mixer_backward",
    )(inner_out, inner_out, y, grad_gated, shared_out, cols, segrow, chan, side, heads)


def on_device(
    resid_in, segments, cotangent, norm_gain, inner_proj, shared_proj, conv_weight, conv_bias,
    dt_offset, rate_log, skip_gain, mix_gain, out_proj,
):
    side_index = lax.axis_index("tensor")
    sides_count = HEADS // (inner_proj.shape[3] // HEADDIM)
    paired = sides_count == 2
    first = side_index == 0
    width = inner_proj.shape[3]
    heads = width // HEADDIM
    length = segments.shape[0]
    rows = length // sides_count
    layers = norm_gain.shape[0]
    chan_start = side_index * width
    head_start = side_index * heads

    def swap(value):
        return lax.ppermute(value, "tensor", [(0, 1), (1, 0)])

    def gather_sides(mine):
        if not paired:
            return lax.all_gather(mine, "tensor", axis=0)
        other = swap(mine)
        return jnp.stack([jnp.where(first, mine, other), jnp.where(first, other, mine)], axis=0)

    def gather_rows(mine):
        return gather_sides(mine).reshape(-1, mine.shape[1])

    def side_sum_of(mine):
        return mine + swap(mine) if paired else lax.psum(mine, "tensor")

    def scatter_sum(part):
        if not paired:
            return lax.psum_scatter(part, "tensor", scatter_dimension=0, tiled=True)
        other = lax.dynamic_slice_in_dim(part, (1 - side_index) * rows, rows, 0)
        mine = lax.dynamic_slice_in_dim(part, side_index * rows, rows, 0)
        return mine + swap(other.astype(bf16)).astype(f32)

    def cut(values, start, size):
        return lax.dynamic_slice_in_dim(values, start, size, values.ndim - 1)

    position = lax.iota(jnp.int32, length)
    columns = []
    for lag in range(1, KCONV):
        columns.append(((jnp.roll(segments, lag) == segments) & (position >= lag)).astype(f32))
    seg_float = segments.astype(f32)
    columns.append(seg_float)
    segrow = jnp.broadcast_to(seg_float[None, :], (8, length))

    def cols_with(inv, coef):
        zero = jnp.zeros((length,), f32)
        return jnp.stack(columns + [inv, coef, zero, zero], axis=1)

    zero = jnp.zeros((length,), f32)
    plain_cols = cols_with(zero, zero)

    inner_ws, out_ws, side_ws, chans, sides, head_rows = [], [], [], [], [], []
    for layer in range(layers):
        inner_ws.append(
            lax.all_gather(inner_proj[layer].reshape(-1, 2 * width), "dp", axis=0, tiled=True)
        )
        out_ws.append(lax.all_gather(out_proj[layer].T, "dp", axis=0, tiled=True))
        shared_w = shared_proj[layer]
        side_ws.append(
            jnp.concatenate(
                [
                    shared_w[:, : 2 * STATE],
                    cut(shared_w, 2 * STATE + head_start, heads),
                    jnp.zeros((D, LANES - heads), bf16),
                ],
                axis=1,
            )
        )
        chans.append(
            jnp.concatenate(
                [
                    cut(conv_weight[layer], chan_start, width),
                    cut(conv_bias[layer], chan_start, width)[None],
                    cut(mix_gain[layer], chan_start, width)[None],
                    jnp.repeat(cut(skip_gain[layer], head_start, heads), HEADDIM)[None],
                    jnp.zeros((1, width), f32),
                ],
                axis=0,
            )
        )
        sides.append(
            jnp.concatenate(
                [
                    conv_weight[layer][:, INNER:],
                    conv_bias[layer][None, INNER:],
                    jnp.zeros((3, 2 * STATE), f32),
                ],
                axis=0,
            )
        )
        head_rows.append(
            jnp.zeros((8, LANES), f32)
            .at[0, :heads].set(cut(dt_offset[layer], head_start, heads))
            .at[1, :heads].set(jnp.exp(cut(rate_log[layer], head_start, heads)))
        )

    stored = []
    residual = resid_in
    for layer in range(layers):
        gain_in = norm_gain[layer]
        inv_in = lax.rsqrt(jnp.mean(residual * residual, axis=1) + epsilon)
        normed = (residual * inv_in[:, None] * gain_in[None, :]).astype(bf16)
        normed_all = gather_rows(normed)
        shared_out = dot(normed_all, side_ws[layer])
        inner_out = dot(normed_all, inner_ws[layer])
        y, mix_pre = mixer_forward(
            inner_out, shared_out, plain_cols, segrow, chans[layer], sides[layer],
            head_rows[layer],
        )
        squares = jnp.sum(mix_pre * mix_pre, axis=1)
        squares = side_sum_of(squares)
        inv_mix = lax.rsqrt(squares / INNER + epsilon)
        gated = (mix_pre * inv_mix[:, None] * chans[layer][5:6]).astype(bf16)
        stored.append((residual, inv_in, normed_all, shared_out, inner_out, y, mix_pre, inv_mix, gated))
        residual = residual + scatter_sum(dot(gated, out_ws[layer], 1, 1))
    layer_output = residual

    grad_resid = cotangent
    results = [None] * layers
    for layer in reversed(range(layers)):
        residual, inv_in, normed_all, shared_out, inner_out, y, mix_pre, inv_mix, gated = stored[layer]
        grad_all = gather_rows(grad_resid.astype(bf16))
        grad_gated = dot(grad_all, out_ws[layer])
        grad_out = dot(grad_all, gated, 0, 0).astype(bf16)
        out_shard = lax.psum_scatter(grad_out, "dp", scatter_dimension=0, tiled=True)
        inner_dot = jnp.sum(grad_gated * chans[layer][5:6] * mix_pre, axis=1)
        inner_dot = side_sum_of(inner_dot)
        coef = inv_mix * inv_mix * inv_mix * inner_dot / INNER
        gz, gx, gshared, gchan, gside, gheads = mixer_backward(
            inner_out, y, grad_gated, shared_out, cols_with(inv_mix, coef), segrow,
            chans[layer], sides[layer], head_rows[layer],
        )
        part = (
            dot(gz, inner_ws[layer][:, :width], 1, 1)
            + dot(gx, inner_ws[layer][:, width:], 1, 1)
            + dot(gshared, side_ws[layer], 1, 1)
        )
        grad_normed = scatter_sum(part)
        grad_side = dot(normed_all, gshared, 0, 0)
        gain_in = norm_gain[layer]
        weighted = grad_normed * gain_in[None, :]
        grad_gain_in = jnp.sum(grad_normed * residual * inv_in[:, None], axis=0)
        input_dot = jnp.sum(weighted * residual, axis=1)
        cubed = inv_in * inv_in * inv_in
        grad_resid = (
            grad_resid + weighted * inv_in[:, None] - residual * (cubed * input_dot / D)[:, None]
        )
        gskip = jnp.sum(gchan[6].reshape(heads, HEADDIM), axis=1)
        small = jnp.concatenate(
            [
                gchan[:6].reshape(-1), gheads[0, :heads], gheads[1, :heads], gskip,
                gside[:5].reshape(-1), grad_gain_in,
            ]
        )
        small_rows = 128 * (-(-small.shape[0] // (128 * SIDE)))
        small = jnp.pad(small, (0, small_rows * SIDE - small.shape[0])).reshape(small_rows, SIDE)
        packed = jnp.concatenate([grad_side, small], axis=0).astype(bf16)
        packed = lax.psum_scatter(packed, "dp", scatter_dimension=0, tiled=True)
        packed = lax.all_gather(packed, "dp", axis=0, tiled=True)
        packed = gather_sides(packed).astype(f32)
        inner_shard = lax.psum_scatter(
            jnp.concatenate([dot(normed_all, gz, 0, 0), dot(normed_all, gx, 0, 0)], axis=1).astype(bf16),
            "dp", scatter_dimension=0, tiled=True,
        )
        summed = jnp.sum(packed, axis=0)
        grad_dt = packed[:, :D, 2 * STATE : 2 * STATE + heads]
        grad_dt = jnp.transpose(grad_dt, (1, 0, 2)).reshape(D, HEADS)
        grad_shared = jnp.concatenate([summed[:D, : 2 * STATE], grad_dt], axis=1)
        flat = packed[:, D:].reshape(sides_count, -1)
        flat_sum = summed[D:].reshape(-1)

        def channels(place):
            return flat[:, place * width : (place + 1) * width].reshape(-1)

        def of_heads(place):
            start = 6 * width + place * heads
            return flat[:, start : start + heads].reshape(-1)

        base = 6 * width + 3 * heads
        side_sum = flat_sum[base : base + 10 * STATE].reshape(5, 2 * STATE)
        conv_x = jnp.stack([channels(k) for k in range(KCONV)], axis=0)
        results[layer] = (
            flat_sum[base + 10 * STATE : base + 10 * STATE + D],
            inner_shard.astype(f32).reshape(-1, 2, width),
            grad_shared,
            jnp.concatenate([conv_x, side_sum[:4]], axis=1),
            jnp.concatenate([channels(4), side_sum[4]], axis=0),
            of_heads(0),
            of_heads(1),
            of_heads(2),
            channels(5),
            out_shard.T.astype(f32),
        )
    stacked = [
        jnp.stack([results[layer][member] for layer in range(layers)], axis=0)
        for member in range(10)
    ]
    return (layer_output, grad_resid, *stacked)


def solution(mesh):
    tokens = P(("dp", "tensor"), None)
    weights = (P(None, "dp", None, "tensor"), P(None, "tensor", "dp"))
    in_specs = (
        tokens, P("dp"), tokens, P(), weights[0], P(), P(), P(), P(), P(), P(), P(), weights[1],
    )
    out_specs = (
        tokens, tokens, P(), weights[0], P(), P(), P(), P(), P(), P(), P(), weights[1],
    )
    return jax.shard_map(
        on_device, mesh=mesh, in_specs=in_specs, out_specs=out_specs, check_vma=False
    )
```

time: 1640 us -> 700 us (0.43)
  waiting for transfers between devices: 841 us -> 354 us
  local copies, waits for them, and re-layouts: 284 us -> 73.5 us
  matrix products: 272 us -> 66.1 us
  other arithmetic: 200 us -> 41.6 us
  Pallas kernels: 0 us -> 74.6 us
  blocking collectives: 19.7 us -> 47.9 us
    reduce_scatter x10 -> x2, waiting for transfers between devices: 469 us -> 48.9 us  [on_device(): lax.psum_scatter(grad_out, 'dp', scatter_dimension=0, tiled=True)]
    psum x2 -> x0, waiting for transfers between devices: 240 us -> none  [on_device(): lax.psum((grad_gain_in, grad_shared_w, conv_grad, offset_grad, place_slot...]
    dot_general x46 -> x22, matrix products: 254 us -> 66.1 us  [dot(): lax.dot_general(a, b, (((ca,), (cb,)), ((), ())), precision=precision, pr...]
    unnamed x20 -> x14, waiting for transfers between devices: 1.01 us -> 162 us
    reshape x49 -> x10, local copies, waits for them, and re-layouts: 105 us -> 3.33 us  [the longest x2 1.39 us: on_device(): gchan[:6].reshape(-1)]
    pallas_call x0 -> x4, Pallas kernels: none -> 74.6 us  [the longest x2 46.5 us: mixer_backward(): pl.pallas_call(backward_kernel, grid=(steps,), in_specs=[lanes_block(leng...]
    ppermute x0 -> x14, waiting for transfers between devices: none -> 73.8 us  [swap(): return lax.ppermute(value, 'tensor', [(0, 1), (1, 0)])]
    all_gather x8 -> x4, waiting for transfers between devices: 131 us -> 69.8 us  [the longest x2 36.2 us: on_device(): out_ws.append(lax.all_gather(out_proj[layer].T, 'dp', axis=0, tiled=True))]
  transfers between devices with their start and end apart: 20 -> 24, of which waited for: 15 -> 19; matrix products, arithmetic and copies ran while one was open for 20% -> 22% of each run, Pallas kernels for 0% -> 7%
where the time goes in v1:
time: 700 us; the launch traced here: 690 us
  waiting for transfers between devices  354 us (51%)
  Pallas kernels  74.6 us (11%)
  local copies, waits for them, and re-layouts  73.5 us (10%)
  matrix products  66.1 us (9%)
  blocking collectives  47.9 us (7%)
  other arithmetic  41.6 us (6%)
  between operations  16.1 us (2%)
  starting transfers between devices  15.9 us (2%)
    unnamed x14, waiting for transfers between devices  162 us
    ppermute x14, waiting for transfers between devices, swap(): return lax.ppermute(value, 'tensor', [(0, 1), (1, 0)])  73.8 us
    dot_general x22, matrix products, dot(): lax.dot_general(a, b, (((ca,), (cb,)), ((), ())), precision=precision, pr...  66.1 us
    reduce_scatter x2, waiting for transfers between devices, on_device(): lax.psum_scatter(grad_out, 'dp', scatter_dimension=0, tiled=True)  48.9 us
    all_gather x2, blocking collectives, on_device(): packed = lax.all_gather(packed, 'dp', axis=0, tiled=True)  47.9 us
    pallas_call x2, Pallas kernels, mixer_backward(): pl.pallas_call(backward_kernel, grid=(steps,), in_specs=[lanes_block(leng...  46.5 us
    unnamed x215, local copies, waits for them, and re-layouts  36.9 us
    all_gather x2, waiting for transfers between devices, on_device(): out_ws.append(lax.all_gather(out_proj[layer].T, 'dp', axis=0, tiled=True))  36.2 us
  transfers between devices with their start and end apart: 24, of which 19 were waited for; matrix products, arithmetic and copies ran while one was open for 22% of the time, Pallas kernels for 7%

profile of v1, /device:TPU:0, one launch (start us, length us, event | category | flops | bytes accessed | tf_op | source)
XLA Modules:
  0.0 689.6 jit_solution(8293816777596805308)
XLA Ops:
  26.1 13.4 %collective-permute-done = bf16[256,1024]{1,0:T(8,128)(2,1)} collective-permute-done((bf16[256,1024]{1,0:T(8,128)(2,1)}, bf16[256,1024]{1,0:T(8,128)(2,1)}, u32[]{:S(2)}, u32[]{:S(2)}) %collective-permute-start) | collective-permute-done | bytes 524320 | tf_op jit(solution)/shard_map/ppermute | solution.py:371
  43.8 20.3 %all-gather.5.cloned.1.call-done = bf16[1024,2048]{1,0:T(8,128)(2,1)} async-done(((bf16[64,2048]{1,0:T(8,128)(2,1)}), bf16[1024,2048]{1,0:T(8,128)(2,1)}) %all-gather.5.cloned.1.call-update) | async-done | bytes 4194320 | tf_op jit(solution)/shard_map/all_gather | solution.py:413
  64.1 6.9 fusion.53.z_ref.x_ref
  71.6 13.9 %mixer_forward.2 = (f32[512,1024]{1,0:T(8,128)}, f32[512,1024]{1,0:T(8,128)}) custom-call(f32[512,2048]{1,0:T(8,128)} %fusion.53.z_ref.x_ref, f32[512,2048]{1,0:T(8,128)} %fusion.53.z_ref.x_ref, f32[512,384]{1,0:T(8,128)} %fusion.9.shared_ref, f32[512,8]{1,0:T(8,128)} %copy.77.cols_ref, f32[8,512]{1,0:T(8,128)} %broadcast_in_dim.10.segrow_ref, ...), custom_call_target="tpu_custom_call" | custom-call | tf_op jit(solution)/shard_map/mixer_forward/pallas_call | solution.py:289
  90.9 15.2 %all-gather.7.cloned.1.call-done = bf16[1024,1024]{1,0:T(8,128)(2,1)} async-done(((bf16[64,1024]{1,0:T(8,128)(2,1)}), bf16[1024,1024]{1,0:T(8,128)(2,1)}) %all-gather.7.cloned.1.call-update) | async-done | bytes 2097168 | tf_op jit(solution)/shard_map/all_gather | solution.py:415
  115.3 11.0 %collective-permute-done.2 = bf16[256,1024]{1,0:T(8,128)(2,1)} collective-permute-done((bf16[256,1024]{1,0:T(8,128)(2,1)}, bf16[256,1024]{1,0:T(8,128)(2,1)}, u32[]{:S(2)}, u32[]{:S(2)}) %collective-permute-start.2) | collective-permute-done | bytes 524320 | tf_op jit(solution)/shard_map/ppermute | solution.py:371
  132.7 8.8 %collective-permute-done.3 = bf16[256,1024]{1,0:T(8,128)(2,1)S(1)} collective-permute-done((bf16[256,1024]{1,0:T(8,128)(2,1)S(1)}, bf16[256,1024]{1,0:T(8,128)(2,1)S(1)}, u32[]{:S(2)}, u32[]{:S(2)}) %collective-permute-start.3) | collective-permute-done | bytes 524320 | tf_op jit(solution)/shard_map/ppermute | solution.py:371
  144.6 13.3 %all-gather.9.cloned.1.call-done = bf16[1024,2048]{1,0:T(8,128)(2,1)} async-done(((bf16[64,2048]{1,0:T(8,128)(2,1)}), bf16[1024,2048]{1,0:T(8,128)(2,1)}) %all-gather.9.cloned.1.call-update) | async-done | bytes 4194320 | tf_op jit(solution)/shard_map/all_gather | solution.py:413
  157.9 6.8 fusion.54.z_ref.x_ref
  164.7 14.1 %mixer_forward.3 = (f32[512,1024]{1,0:T(8,128)}, f32[512,1024]{1,0:T(8,128)}) custom-call(f32[512,2048]{1,0:T(8,128)} %fusion.54.z_ref.x_ref, f32[512,2048]{1,0:T(8,128)} %fusion.54.z_ref.x_ref, f32[512,384]{1,0:T(8,128)} %fusion.8.shared_ref, f32[512,8]{1,0:T(8,128)} %copy.77.cols_ref, f32[8,512]{1,0:T(8,128)} %broadcast_in_dim.10.segrow_ref, ...), custom_call_target="tpu_custom_call" | custom-call | tf_op jit(solution)/shard_map/mixer_forward/pallas_call | solution.py:289
  178.8 21.0 %all-gather.11.cloned.1.call-done = bf16[1024,1024]{1,0:T(8,128)(2,1)} async-done(((bf16[64,1024]{1,0:T(8,128)(2,1)}), bf16[1024,1024]{1,0:T(8,128)(2,1)}) %all-gather.11.cloned.1.call-update) | async-done | bytes 2097168 | tf_op jit(solution)/shard_map/all_gather | solution.py:415
  211.0 23.3 %mixer_backward.2 = (bf16[512,1024]{1,0:T(8,128)(2,1)}, bf16[512,1024]{1,0:T(8,128)(2,1)}, bf16[512,384]{1,0:T(8,128)(2,1)}, f32[8,1024]{1,0:T(8,128)}, f32[8,256]{1,0:T(8,128)}, /*index=5*/f32[8,128]{1,0:T(8,128)}) custom-call(f32[512,2048]{1,0:T(8,128)} %fusion.54.z_ref.x_ref, f32[512,2048]{1,0:T(8,128)} %fusion.54.z_ref.x_ref, ...), custom_call_target="tpu_custom_call" | custom-call | tf_op jit(solution)/shard_map/mixer_backward/pallas_call | solution.py:316
  243.7 11.3 %collective-permute-done.8 = bf16[256,1024]{1,0:T(8,128)(2,1)S(1)} collective-permute-done((bf16[256,1024]{1,0:T(8,128)(2,1)S(1)}, bf16[256,1024]{1,0:T(8,128)(2,1)S(1)}, u32[]{:S(2)}, u32[]{:S(2)}) %collective-permute-start.8) | collective-permute-done | bytes 524320 | tf_op jit(solution)/shard_map/ppermute | solution.py:371
  256.0 8.1 %collective-permute-done.5 = bf16[256,1024]{1,0:T(8,128)(2,1)S(1)} collective-permute-done((bf16[256,1024]{1,0:T(8,128)(2,1)S(1)}, bf16[256,1024]{1,0:T(8,128)(2,1)S(1)}, u32[]{:S(2)}, u32[]{:S(2)}) %collective-permute-start.5) | collective-permute-done | bytes 524320 | tf_op jit(solution)/shard_map/ppermute | solution.py:371
  269.0 8.9 %collective-permute-done.9 = bf16[256,1024]{1,0:T(8,128)(2,1)S(1)} collective-permute-done((bf16[256,1024]{1,0:T(8,128)(2,1)}, bf16[256,1024]{1,0:T(8,128)(2,1)S(1)}, u32[]{:S(2)}, u32[]{:S(2)}) %collective-permute-start.9) | collective-permute-done | bytes 524320 | tf_op jit(solution)/shard_map/ppermute | solution.py:371
  286.4 23.2 %mixer_backward.3 = (bf16[512,1024]{1,0:T(8,128)(2,1)}, bf16[512,1024]{1,0:T(8,128)(2,1)}, bf16[512,384]{1,0:T(8,128)(2,1)}, f32[8,1024]{1,0:T(8,128)}, f32[8,256]{1,0:T(8,128)}, /*index=5*/f32[8,128]{1,0:T(8,128)}) custom-call(f32[512,2048]{1,0:T(8,128)} %fusion.53.z_ref.x_ref, f32[512,2048]{1,0:T(8,128)} %fusion.53.z_ref.x_ref, ...), custom_call_target="tpu_custom_call" | custom-call | tf_op jit(solution)/shard_map/mixer_backward/pallas_call | solution.py:316
  347.0 6.5 copy.98
  357.8 24.5 %all_gather.23 = bf16[1152,384]{1,0:T(8,128)(2,1)} all-gather(bf16[72,384]{1,0:T(8,128)(2,1)} %reduce-scatter.25.cloned.1.call-done), channel_id=1, replica_groups=mesh['dp'=16,'tensor'=2] {'dp'}, dimensions={0}, use_global_device_ids=true | all-gather | bytes 940032 | tf_op jit(solution)/shard_map/all_gather | solution.py:517
  385.5 13.8 %reduce-scatter.23.cloned.1.call-done = bf16[72,384]{1,0:T(8,128)(2,1)} async-done(((bf16[1152,384]{1,0:T(8,128)(2,1)}), bf16[72,384]{1,0:T(8,128)(2,1)}) %reduce-scatter.23.cloned.1.call-update) | async-done | bytes 55312
  399.2 23.5 %all_gather.22 = bf16[1152,384]{1,0:T(8,128)(2,1)} all-gather(bf16[72,384]{1,0:T(8,128)(2,1)} %reduce-scatter.23.cloned.1.call-done), channel_id=1, replica_groups=mesh['dp'=16,'tensor'=2] {'dp'}, dimensions={0}, use_global_device_ids=true | all-gather | bytes 940032 | tf_op jit(solution)/shard_map/all_gather | solution.py:517
  431.8 6.6 copy.96
  479.5 48.9 %reduce-scatter.15.cloned.1.call-done = bf16[64,1024]{1,0:T(8,128)(2,1)} async-done(((bf16[1024,1024]{1,0:T(8,128)(2,1)}), bf16[64,1024]{1,0:T(8,128)(2,1)}) %reduce-scatter.15.cloned.1.call-update) | async-done | bytes 131088 | tf_op jit(solution)/shard_map/reduce_scatter | solution.py:483
  530.2 73.5 %reduce-scatter.21.cloned.1.call-done = bf16[64,2048]{1,0:T(8,128)(2,1)} async-done(((bf16[1024,2048]{1,0:T(8,128)(2,1)}), bf16[64,2048]{1,0:T(8,128)(2,1)}) %reduce-scatter.21.cloned.1.call-update) | async-done | bytes 262160
  605.2 74.1 %reduce-scatter.19.cloned.1.call-done = bf16[64,2048]{1,0:T(8,128)(2,1)} async-done(((bf16[1024,2048]{1,0:T(8,128)(2,1)}), bf16[64,2048]{1,0:T(8,128)(2,1)}) %reduce-scatter.19.cloned.1.call-update) | async-done | bytes 262160
  (451 shorter events, 182.6 us)
Async XLA Ops:
  7.2 56.9 %all-gather.5.cloned.1.call-start = ((), (), s32[]{:S(2)}) async-start(), calls=%async_computation.6 | async-start | bytes 4456448 | tf_op jit(solution)/shard_map/all_gather | solution.py:413
  9.5 96.7 %all-gather.7.cloned.1.call-start = ((), (), s32[]{:S(2)}) async-start(), calls=%async_computation.7 | async-start | bytes 2228224 | tf_op jit(solution)/shard_map/all_gather | solution.py:415
  11.3 146.6 %all-gather.9.cloned.1.call-start = ((), (), s32[]{:S(2)}) async-start(), calls=%async_computation.8 | async-start | bytes 4456448 | tf_op jit(solution)/shard_map/all_gather | solution.py:413
  12.2 187.6 %all-gather.11.cloned.1.call-start = ((), (), s32[]{:S(2)}) async-start(), calls=%async_computation.9 | async-start | bytes 2228224 | tf_op jit(solution)/shard_map/all_gather | solution.py:415
  13.1 117.3 %collective-permute-start.6 = (bf16[256,1024]{1,0:T(8,128)(2,1)}, bf16[256,1024]{1,0:T(8,128)(2,1)}, u32[]{:S(2)}, u32[]{:S(2)}) collective-permute-start(bf16[256,1024]{1,0:T(8,128)(2,1)} %convert_element_type.86), channel_id=1, source_target_pairs={{0,1},{1,0},{2,3},{3,2},{4,5},{5,4},{6,7},{7,6},{8,9},{9,8},{10,11... | collective-permute-start | bytes 1572872 | tf_op jit(solution)/shard_map/ppermute | solution.py:371
  17.2 22.3 %collective-permute-start = (bf16[256,1024]{1,0:T(8,128)(2,1)}, bf16[256,1024]{1,0:T(8,128)(2,1)}, u32[]{:S(2)}, u32[]{:S(2)}) collective-permute-start(bf16[256,1024]{1,0:T(8,128)(2,1)} %multiply_convert_fusion.3), channel_id=1, source_target_pairs={{0,1},{1,0},{2,3},{3,2},{4,5},{5,4},{6,7},{7,6},{8,9},{9,8},{10,11... | collective-permute-start | bytes 1572872 | tf_op jit(solution)/shard_map/ppermute | solution.py:371
  17.3 340.5 %reduce-scatter.25.cloned.1.call-start = ((), (), s32[]{:S(2)}) async-start(), calls=%async_computation.15 | async-start | bytes 940032
  87.3 3.6 collective-permute-start.1
  111.9 14.4 %collective-permute-start.2 = (bf16[256,1024]{1,0:T(8,128)(2,1)}, bf16[256,1024]{1,0:T(8,128)(2,1)}, u32[]{:S(2)}, u32[]{:S(2)}) collective-permute-start(bf16[256,1024]{1,0:T(8,128)(2,1)} %dynamic-slice_convert_fusion.3), channel_id=1, source_target_pairs={{0,1},{1,0},{2,3},{3,2},{4,5},{5,4},{6,7},{7,6},{8,9},{9,8},{10,11... | collective-permute-start | bytes 1572872 | tf_op jit(solution)/shard_map/ppermute | solution.py:371
  128.1 13.3 %collective-permute-start.3 = (bf16[256,1024]{1,0:T(8,128)(2,1)S(1)}, bf16[256,1024]{1,0:T(8,128)(2,1)S(1)}, u32[]{:S(2)}, u32[]{:S(2)}) collective-permute-start(bf16[256,1024]{1,0:T(8,128)(2,1)S(1)} %multiply_convert_fusion.2), channel_id=1, source_target_pairs={{0,1},{1,0},{2,3},{3,2},{4,5},{5,4},{6,7},{7,6},{8,9},{9,8},{10,11... | collective-permute-start | bytes 1572872 | tf_op jit(solution)/shard_map/ppermute | solution.py:371
  205.0 3.6 collective-permute-start.7
  206.5 3.6 collective-permute-start.4
  240.1 14.9 %collective-permute-start.8 = (bf16[256,1024]{1,0:T(8,128)(2,1)S(1)}, bf16[256,1024]{1,0:T(8,128)(2,1)S(1)}, u32[]{:S(2)}, u32[]{:S(2)}) collective-permute-start(bf16[256,1024]{1,0:T(8,128)(2,1)S(1)} %dynamic-slice_convert_fusion.1), channel_id=1, source_target_pairs={{0,1},{1,0},{2,3},{3,2},{4,5},{5,4},{6,7},{7,6},{8,9},{9,8},{10,11... | collective-permute-start | bytes 1572872 | tf_op jit(solution)/shard_map/ppermute | solution.py:371
  242.8 21.3 %collective-permute-start.5 = (bf16[256,1024]{1,0:T(8,128)(2,1)S(1)}, bf16[256,1024]{1,0:T(8,128)(2,1)S(1)}, u32[]{:S(2)}, u32[]{:S(2)}) collective-permute-start(bf16[256,1024]{1,0:T(8,128)(2,1)S(1)} %dynamic-slice_convert_fusion.2), channel_id=1, source_target_pairs={{0,1},{1,0},{2,3},{3,2},{4,5},{5,4},{6,7},{7,6},{8,9},{9,8},{10,11... | collective-permute-start | bytes 1572872 | tf_op jit(solution)/shard_map/ppermute | solution.py:371
  265.9 11.9 %collective-permute-start.9 = (bf16[256,1024]{1,0:T(8,128)(2,1)}, bf16[256,1024]{1,0:T(8,128)(2,1)S(1)}, u32[]{:S(2)}, u32[]{:S(2)}) collective-permute-start(bf16[256,1024]{1,0:T(8,128)(2,1)} %get-tuple-element.134), channel_id=1, source_target_pairs={{0,1},{1,0},{2,3},{3,2},{4,5},{5,4},{6,7},{7,6},{8,9},{9,8},{10,11... | collective-permute-start | bytes 1572872 | tf_op jit(solution)/shard_map/ppermute | solution.py:371
  281.8 3.7 collective-permute-start.10
  283.5 115.7 %reduce-scatter.23.cloned.1.call-start = ((), (), s32[]{:S(2)}) async-start(), calls=%async_computation.14 | async-start | bytes 940032
  316.1 9.9 %collective-permute-start.11 = (bf16[256,1024]{1,0:T(8,128)(2,1)}, bf16[256,1024]{1,0:T(8,128)(2,1)}, u32[]{:S(2)}, u32[]{:S(2)}) collective-permute-start(bf16[256,1024]{1,0:T(8,128)(2,1)} %dynamic-slice_convert_fusion), channel_id=1, source_target_pairs={{0,1},{1,0},{2,3},{3,2},{4,5},{5,4},{6,7},{7,6},{8,9},{9,8},{10,11... | collective-permute-start | bytes 1572872 | tf_op jit(solution)/shard_map/ppermute | solution.py:371
  329.9 149.7 %reduce-scatter.17.cloned.1.call-start = ((), (), s32[]{:S(2)}) async-start(), calls=%async_computation.11 | async-start | bytes 2228224 | tf_op jit(solution)/shard_map/reduce_scatter | solution.py:483
  334.6 193.8 %reduce-scatter.15.cloned.1.call-start = ((), (), s32[]{:S(2)}) async-start(), calls=%async_computation.10 | async-start | bytes 2228224 | tf_op jit(solution)/shard_map/reduce_scatter | solution.py:483
  339.9 263.8 %reduce-scatter.21.cloned.1.call-start = ((), (), s32[]{:S(2)}) async-start(), calls=%async_computation.13 | async-start | bytes 4456448
  353.6 325.7 %reduce-scatter.19.cloned.1.call-start = ((), (), s32[]{:S(2)}) async-start(), calls=%async_computation.12 | async-start | bytes 4456448
  384.5 57.4 %collective-permute-start.13 = (bf16[1152,384]{0,1:T(8,128)(2,1)}, bf16[1152,384]{0,1:T(8,128)(2,1)}, u32[]{:S(2)}, u32[]{:S(2)}) collective-permute-start(bf16[1152,384]{0,1:T(8,128)(2,1)} %copy.86), channel_id=1, source_target_pairs={{0,1},{1,0},{2,3},{3,2},{4,5},{5,4},{6,7},{7,6},{8,9},{9,8},{10,11... | collective-permute-start | bytes 2654216 | tf_op jit(solution)/shard_map/ppermute | solution.py:371
  424.9 22.2 %collective-permute-start.12 = (bf16[1152,384]{0,1:T(8,128)(2,1)}, bf16[1152,384]{0,1:T(8,128)(2,1)}, u32[]{:S(2)}, u32[]{:S(2)}) collective-permute-start(bf16[1152,384]{0,1:T(8,128)(2,1)} %copy.82), channel_id=1, source_target_pairs={{0,1},{1,0},{2,3},{3,2},{4,5},{5,4},{6,7},{7,6},{8,9},{9,8},{10,11... | collective-permute-start | bytes 2654216 | tf_op jit(solution)/shard_map/ppermute | solution.py:371
  (97 other events, 1375.9 us)
Sparse Core Ops, SparseCore 0:
  10.8 53.2 all-gather.4
  66.2 39.8 all-gather.6
  108.3 49.4 all-gather.8
  159.9 39.8 all-gather.10
  283.6 54.9 reduce-scatter.24
  342.1 57.0 reduce-scatter.22
  403.0 60.6 reduce-scatter.16
  467.8 60.5 reduce-scatter.14
  532.3 71.4 reduce-scatter.20
  607.9 71.3 reduce-scatter.18
